TPU v7x, 32 devices: a whole 2x2x4 slice. The times are simulated.
32 devices in a mesh: items: 4 (over y, x), seq: 8 (over z, core).
Axes of the slice: x: 2, y: 2, z: 4, core: 2. Of those that a mesh axis runs over, the one named last changes fastest.
Arguments:
- tokens: bfloat16 [4, 2048, 1024], P('items', 'seq'), may hold values from -6 to 6
- decay_rate: float32 [8], replicated, may hold values from 0.96 to 1, as said below
- query_weight: bfloat16 [1024, 1024], P(('items', 'seq')), may hold values from -0.1875 to 0.1875
- key_weight: bfloat16 [1024, 1024], P(('items', 'seq')), may hold values from -0.1875 to 0.1875
- value_weight: bfloat16 [1024, 1024], P(('items', 'seq')), may hold values from -0.1875 to 0.1875
- update_weight: bfloat16 [1024, 1024], P(('items', 'seq')), may hold values from -0.1875 to 0.1875
- output_weight: bfloat16 [1024, 1024], P(('items', 'seq')), may hold values from -0.1875 to 0.1875
- gate_weight: bfloat16 [1024, 2816], P(('items', 'seq')), may hold values from -0.1875 to 0.1875
- up_weight: bfloat16 [1024, 2816], P(('items', 'seq')), may hold values from -0.1875 to 0.1875
- down_weight: bfloat16 [2816, 1024], P(None, ('items', 'seq')), may hold values from -0.109375 to 0.109375
- cotangent: bfloat16 [4, 2048, 1024], P('items', 'seq'), may hold values from -6 to 6
Outputs:
- mixed: bfloat16 [4, 2048, 1024], P('items', 'seq')
- tokens_grad: float32 [4, 2048, 1024], P('items', 'seq')
- query_grad: float32 [1024, 1024], P(('items', 'seq'))
- key_grad: float32 [1024, 1024], P(('items', 'seq'))
- value_grad: float32 [1024, 1024], P(('items', 'seq'))
- update_grad: float32 [1024, 1024], P(('items', 'seq'))
- output_grad: float32 [1024, 1024], P(('items', 'seq'))
- gate_grad: float32 [1024, 2816], P(('items', 'seq'))
- up_grad: float32 [1024, 2816], P(('items', 'seq'))
- down_grad: float32 [2816, 1024], P(None, ('items', 'seq'))
Inputs may be any that keep to these rules, and one draw needn't show every extreme that they name: decay_rate[h] is lambda_h, the factor by which head h keeps its state from one position to the next.
All inputs are finite; a program needn't handle non-finite values.
Results may differ from a plain program's by a relative error of at most 0.015.
Values may be sent and summed in bfloat16 or wider, within the bound.
No kernel may reach another device: no remote copies, remote signals or barrier semaphores. Data moves between devices by JAX's collectives and lax.ppermute only.
A program may use at most 320 MiB of HBM per device.

v0:
```python
import math

import jax
import jax.numpy as jnp
from jax import lax
from jax.sharding import PartitionSpec as P

epsilon = 1e-06


def entering(value, axis, join, neutral, backward):
    count, mine = (lax.axis_size(axis), lax.axis_index(axis))
    pieces = jax.tree.map(lambda part: lax.all_gather(part, axis), value)
    if backward:
        pieces = jax.tree.map(lambda part: part[::-1], pieces)
        mine = count - 1 - mine
    running = jax.tree.map(
        lambda part, zero: jnp.full_like(part, 0) + jnp.asarray(zero, part.dtype), value, neutral
    )

    def step(position, running):
        longer = join(running, jax.tree.map(lambda part: part[position], pieces))
        return jax.tree.map(lambda new, old: jnp.where(position < mine, new, old), longer, running)

    return lax.fori_loop(0, count - 1, step, running)


def product(left_op, right_op):
    return jnp.dot(left_op, right_op, preferred_element_type=jnp.float32)


def outer_sum(left_op, right_op):
    return lax.dot_general(
        left_op, right_op, (((0,), (0,)), ((), ())), preferred_element_type=jnp.float32
    )


def inner_back(left_op, right_op):
    return lax.dot_general(
        left_op, right_op, (((1,), (1,)), ((), ())), preferred_element_type=jnp.float32
    )


def norm_factor(values_in):
    return lax.rsqrt(jnp.mean(values_in * values_in, axis=-1, keepdims=True) + epsilon)


def norm_back(normed, norm_rs, grad_in):
    return norm_rs * (grad_in - normed * jnp.mean(grad_in * normed, axis=-1, keepdims=True))


def rotation_tables(positions, head_size):
    half_width = head_size // 2
    pair_index = jnp.arange(half_width, dtype=jnp.int32)
    step_sizes = jnp.right_shift(jnp.full((half_width,), 8192, jnp.int32), pair_index // 5)
    phase_int = positions[:, None] * step_sizes[None, :] % 65536
    angles = phase_int.astype(jnp.float32) * (2.0 * math.pi / 65536.0)
    return (jnp.cos(angles), jnp.sin(angles))


def rotate(values_in, cosine, sine_tab):
    half_width = values_in.shape[-1] // 2
    first_half = values_in[..., :half_width]
    second_half = values_in[..., half_width:]
    wide_cos = cosine[:, None, :]
    wide_sin = sine_tab[:, None, :]
    return jnp.concatenate(
        [
            first_half * wide_cos - second_half * wide_sin,
            first_half * wide_sin + second_half * wide_cos,
        ],
        axis=-1,
    )


def decayed_combine(earlier, latter):
    return (earlier[0] * latter[0], latter[0][..., None, None] * earlier[1] + latter[1])


def body(
    tokens,
    decay_rate,
    query_weight,
    key_weight,
    value_weight,
    update_weight,
    output_weight,
    gate_weight,
    up_weight,
    down_weight,
    cotangent,
):
    query_w, key_w, value_w, update_w, output_w, gate_w, up_w, down_w = (
        lax.all_gather(query_weight, ("items", "seq"), axis=0, tiled=True),
        lax.all_gather(key_weight, ("items", "seq"), axis=0, tiled=True),
        lax.all_gather(value_weight, ("items", "seq"), axis=0, tiled=True),
        lax.all_gather(update_weight, ("items", "seq"), axis=0, tiled=True),
        lax.all_gather(output_weight, ("items", "seq"), axis=0, tiled=True),
        lax.all_gather(gate_weight, ("items", "seq"), axis=0, tiled=True),
        lax.all_gather(up_weight, ("items", "seq"), axis=0, tiled=True),
        lax.all_gather(down_weight, ("items", "seq"), axis=1, tiled=True),
    )
    model_width = tokens.shape[-1]
    head_count = decay_rate.shape[0]
    head_size = model_width // head_count
    inner_width = gate_w.shape[1]
    inputs = tokens.reshape(-1, model_width).astype(jnp.float32)
    tok_rows = inputs.shape[0]
    head_shape = (tok_rows, head_count, head_size)
    scale_in = norm_factor(inputs)
    normed_in = inputs * scale_in
    normed_low = normed_in.astype(jnp.bfloat16)
    query_pre = product(normed_low, query_w)
    key_pre = product(normed_low, key_w)
    value_low = product(normed_low, value_w).astype(jnp.bfloat16).reshape(head_shape)
    update = product(normed_low, update_w).reshape(head_shape)
    positions = lax.axis_index("seq") * tok_rows + jnp.arange(tok_rows, dtype=jnp.int32)
    cosine, sine_tab = rotation_tables(positions, head_size)
    query_sig = jax.nn.sigmoid(query_pre)
    key_sig = jax.nn.sigmoid(key_pre)
    query_act = rotate((query_pre * query_sig).reshape(head_shape), cosine, sine_tab)
    key_act = rotate((key_pre * key_sig).reshape(head_shape), cosine, sine_tab)
    log_decay = jnp.log(decay_rate)
    local_pos = jnp.arange(tok_rows).astype(jnp.float32)
    query_decay = jnp.exp(log_decay[None, :] * (local_pos[:, None] + 1.0))[:, :, None]
    key_decay = jnp.exp(log_decay[None, :] * (tok_rows - 1.0 - local_pos[:, None]))[:, :, None]
    offset = local_pos[:, None] - local_pos[None, :]
    decay_mask = jnp.where(
        offset >= 0.0, jnp.exp(log_decay[:, None, None] * jnp.maximum(offset, 0.0)[None]), 0.0
    )
    queries = query_act.astype(jnp.bfloat16)
    keys = key_act.astype(jnp.bfloat16)
    query_scaled = (query_act * query_decay).astype(jnp.bfloat16)
    key_scaled = (key_act * key_decay).astype(jnp.bfloat16)
    scores = jnp.einsum("the,she->hts", queries, keys, preferred_element_type=jnp.float32)
    weight_low = (scores * decay_mask).astype(jnp.bfloat16)
    intra = jnp.einsum("hts,she->the", weight_low, value_low, preferred_element_type=jnp.float32)
    local_state = jnp.einsum(
        "she,shf->hef", key_scaled, value_low, preferred_element_type=jnp.float32
    )
    factor = jnp.exp(log_decay * tok_rows)
    identity = (jnp.ones_like(factor), jnp.zeros_like(local_state))
    _, prefix = entering((factor, local_state), "seq", decayed_combine, identity, False)
    prefix_low = prefix.astype(jnp.bfloat16)
    inter = jnp.einsum("the,hef->thf", query_scaled, prefix_low, preferred_element_type=jnp.float32)
    attn_raw = intra + inter
    scale_heads = norm_factor(attn_raw)
    normed_heads = attn_raw * scale_heads
    mixed_low = (normed_heads * update).reshape(tok_rows, model_width).astype(jnp.bfloat16)
    attn_out = product(mixed_low, output_w)
    resid = inputs + attn_out
    scale_mid = norm_factor(resid)
    normed_mid = resid * scale_mid
    mid_low = normed_mid.astype(jnp.bfloat16)
    gate_act = product(mid_low, gate_w)
    up_act = product(mid_low, up_w)
    hidden_low = (gate_act * up_act).astype(jnp.bfloat16)
    ffn_out = product(hidden_low, down_w)
    mixed = (resid + ffn_out).astype(jnp.bfloat16).reshape(tokens.shape)
    grad_ffn = cotangent.reshape(tok_rows, model_width)
    grad_out = grad_ffn.astype(jnp.float32)
    grad_hidden = inner_back(grad_ffn, down_w)
    grad_gate = (grad_hidden * up_act).astype(jnp.bfloat16)
    grad_up = (grad_hidden * gate_act).astype(jnp.bfloat16)
    grad_mid = inner_back(grad_gate, gate_w) + inner_back(grad_up, up_w)
    grad_resid = grad_out + norm_back(normed_mid, scale_mid, grad_mid)
    grad_attn = grad_resid.astype(jnp.bfloat16)
    grad_mixed = inner_back(grad_attn, output_w).reshape(head_shape)
    grad_update = (grad_mixed * normed_heads).reshape(tok_rows, model_width).astype(jnp.bfloat16)
    grad_raw = norm_back(normed_heads, scale_heads, grad_mixed * update).astype(jnp.bfloat16)
    grad_weight = jnp.einsum(
        "the,she->hts", grad_raw, value_low, preferred_element_type=jnp.float32
    )
    grad_scores = (grad_weight * decay_mask).astype(jnp.bfloat16)
    grad_query = jnp.einsum("hts,she->the", grad_scores, keys, preferred_element_type=jnp.float32)
    grad_key = jnp.einsum("hts,the->she", grad_scores, queries, preferred_element_type=jnp.float32)
    grad_value = jnp.einsum(
        "hts,the->she", weight_low, grad_raw, preferred_element_type=jnp.float32
    )
    grad_qscaled = jnp.einsum(
        "thf,hef->the", grad_raw, prefix_low, preferred_element_type=jnp.float32
    )
    grad_prefix = jnp.einsum(
        "the,thf->hef", query_scaled, grad_raw, preferred_element_type=jnp.float32
    )
    _, grad_state = entering((factor, grad_prefix), "seq", decayed_combine, identity, True)
    state_low = grad_state.astype(jnp.bfloat16)
    grad_kscaled = jnp.einsum(
        "hef,shf->she", state_low, value_low, preferred_element_type=jnp.float32
    )
    grad_value = grad_value + jnp.einsum(
        "she,hef->shf", key_scaled, state_low, preferred_element_type=jnp.float32
    )
    grad_value_low = grad_value.reshape(tok_rows, model_width).astype(jnp.bfloat16)
    grad_qact = grad_query + grad_qscaled * query_decay
    grad_kact = grad_key + grad_kscaled * key_decay
    grad_qswish = rotate(grad_qact, cosine, -sine_tab).reshape(tok_rows, model_width)
    grad_kswish = rotate(grad_kact, cosine, -sine_tab).reshape(tok_rows, model_width)
    grad_qpre = (grad_qswish * query_sig * (1.0 + query_pre * (1.0 - query_sig))).astype(
        jnp.bfloat16
    )
    grad_kpre = (grad_kswish * key_sig * (1.0 + key_pre * (1.0 - key_sig))).astype(jnp.bfloat16)
    grad_norm_in = (
        inner_back(grad_qpre, query_w)
        + inner_back(grad_kpre, key_w)
        + inner_back(grad_value_low, value_w)
        + inner_back(grad_update, update_w)
    )
    tokens_grad = (grad_resid + norm_back(normed_in, scale_in, grad_norm_in)).reshape(tokens.shape)
    owned = lax.psum_scatter(
        jnp.concatenate(
            [
                outer_sum(normed_low, grad_qpre),
                outer_sum(normed_low, grad_kpre),
                outer_sum(normed_low, grad_value_low),
                outer_sum(normed_low, grad_update),
                outer_sum(mixed_low, grad_attn),
                outer_sum(mid_low, grad_gate),
                outer_sum(mid_low, grad_up),
                outer_sum(grad_ffn, hidden_low),
            ],
            axis=1,
        ),
        ("items", "seq"),
        scatter_dimension=0,
        tiled=True,
    )
    query_o = owned[:, 0:model_width]
    key_o = owned[:, model_width : 2 * model_width]
    value_o = owned[:, 2 * model_width : 3 * model_width]
    update_o = owned[:, 3 * model_width : 4 * model_width]
    output_o = owned[:, 4 * model_width : 5 * model_width]
    gate_o = owned[:, 5 * model_width : 5 * model_width + inner_width]
    up_o = owned[:, 5 * model_width + inner_width : 5 * model_width + 2 * inner_width]
    down_o = owned[:, 5 * model_width + 2 * inner_width : 5 * model_width + 3 * inner_width].T
    return (mixed, tokens_grad, query_o, key_o, value_o, update_o, output_o, gate_o, up_o, down_o)


def solution(mesh):
    placed = (
        P("items", "seq", None),
        P(),
        P(("items", "seq"), None),
        P(("items", "seq"), None),
        P(("items", "seq"), None),
        P(("items", "seq"), None),
        P(("items", "seq"), None),
        P(("items", "seq"), None),
        P(("items", "seq"), None),
        P(None, ("items", "seq")),
        P("items", "seq", None),
    )
    return jax.shard_map(
        body,
        mesh=mesh,
        in_specs=placed,
        out_specs=(
            P("items", "seq", None),
            P("items", "seq", None),
            P(("items", "seq"), None),
            P(("items", "seq"), None),
            P(("items", "seq"), None),
            P(("items", "seq"), None),
            P(("items", "seq"), None),
            P(("items", "seq"), None),
            P(("items", "seq"), None),
            P(None, ("items", "seq")),
        ),
        check_vma=False,
    )
```

profile of v0, /device:TPU:0, one launch (start us, length us, event | category | flops | bytes accessed | tf_op | source)
XLA Modules:
  0.0 1275.7 jit_solution(9859914472912682649)
XLA Ops:
  10.1 1.2 dynamic-slice
  12.0 1.2 fusion.21
  15.2 55.0 %all-gather.18.cloned.1.call-done = bf16[1024,1024]{1,0:T(8,128)(2,1)} async-done(((bf16[32,1024]{1,0:T(8,128)(2,1)}), bf16[1024,1024]{1,0:T(8,128)(2,1)}) %all-gather.18.cloned.1.call-update) | async-done | bytes 2097168 | tf_op jit(solution)/shard_map/all_gather | solution.py:95
  70.2 2.5 fusion.67
  74.3 54.3 %all-gather.16.cloned.1.call-done = bf16[1024,1024]{1,0:T(8,128)(2,1)} async-done(((bf16[32,1024]{1,0:T(8,128)(2,1)}), bf16[1024,1024]{1,0:T(8,128)(2,1)}) %all-gather.16.cloned.1.call-update) | async-done | bytes 2097168 | tf_op jit(solution)/shard_map/all_gather | solution.py:94
  128.6 2.3 fusion.69
  135.3 51.6 %all-gather.14.cloned.1.call-done = bf16[1024,1024]{1,0:T(8,128)(2,1)} async-done(((bf16[32,1024]{1,0:T(8,128)(2,1)}), bf16[1024,1024]{1,0:T(8,128)(2,1)}) %all-gather.14.cloned.1.call-update) | async-done | bytes 2097168 | tf_op jit(solution)/shard_map/all_gather | solution.py:96
  186.9 2.4 fusion.14
  194.1 15.6 %all-reduce = f32[64]{0:T(128)S(1)} all-reduce(f32[64]{0:T(128)S(1)} %copy-done.55), channel_id=2, replica_groups=mesh['items'=4,'seq'=8] {'seq'}, use_global_device_ids=true, to_apply=%add | all-reduce | flops 64 | bytes 512
  210.8 34.3 %all-gather.20.cloned.1.call-done = bf16[1024,1024]{1,0:T(8,128)(2,1)} async-done(((bf16[32,1024]{1,0:T(8,128)(2,1)}), bf16[1024,1024]{1,0:T(8,128)(2,1)}) %all-gather.20.cloned.1.call-update) | async-done | bytes 2097168 | tf_op jit(solution)/shard_map/all_gather | solution.py:97
  245.1 4.0 copy.60
  249.1 2.0 fusion.40
  251.1 1.4 multiply_convert_fusion.8
  254.6 38.0 %all-gather.30.cloned.1.call-done = f32[64,128,128]{2,1,0:T(8,128)} async-done(((f32[8,128,128]{2,1,0:T(8,128)}), f32[64,128,128]{2,1,0:T(8,128)}) %all-gather.30.cloned.1.call-update) | async-done | bytes 4194320 | tf_op jit(solution)/shard_map/all_gather | solution.py:13
  292.7 8.7 while.28
  292.7 1.2 fusion.135
  293.9 1.2 fusion.135
  295.1 1.2 fusion.135
  296.4 1.2 fusion.135
  297.6 1.2 fusion.135
  298.8 1.2 fusion.135
  300.0 1.2 fusion.135
  303.4 1.8 multiply_convert_fusion.7
  305.2 45.5 %all-gather.22.cloned.1.call-done = bf16[1024,1024]{1,0:T(8,128)(2,1)} async-done(((bf16[32,1024]{1,0:T(8,128)(2,1)}), bf16[1024,1024]{1,0:T(8,128)(2,1)}) %all-gather.22.cloned.1.call-update) | async-done | bytes 2097168 | tf_op jit(solution)/shard_map/all_gather | solution.py:98
  350.7 2.4 multiply_reduce_fusion.2
  353.3 66.4 %all-gather.26.cloned.1.call-done = bf16[1024,2816]{1,0:T(8,128)(2,1)} async-done(((bf16[32,2816]{1,0:T(8,128)(2,1)}), bf16[1024,2816]{1,0:T(8,128)(2,1)}) %all-gather.26.cloned.1.call-update) | async-done | bytes 5767184 | tf_op jit(solution)/shard_map/all_gather | solution.py:100
  419.7 5.9 fusion.76
  425.6 63.3 %all-gather.24.cloned.1.call-done = bf16[1024,2816]{1,0:T(8,128)(2,1)} async-done(((bf16[32,2816]{1,0:T(8,128)(2,1)}), bf16[1024,2816]{1,0:T(8,128)(2,1)}) %all-gather.24.cloned.1.call-update) | async-done | bytes 5767184 | tf_op jit(solution)/shard_map/all_gather | solution.py:99
  488.8 5.8 fusion.75
  494.7 63.3 %all-gather.28.cloned.1.call-done = bf16[2816,1024]{0,1:T(8,128)(2,1)} async-done(((bf16[2816,32]{0,1:T(8,128)(2,1)}), bf16[2816,1024]{0,1:T(8,128)(2,1)}) %all-gather.28.cloned.1.call-update) | async-done | bytes 5767184 | tf_op jit(solution)/shard_map/all_gather | solution.py:101
  558.0 7.1 multiply_convert_fusion
  565.2 1.7 fusion.77
  566.9 4.5 multiply_reduce_fusion.1
  571.7 1.2 copy-done.14
  576.6 1.2 fusion.79
  577.9 1.9 multiply_convert_fusion.3
  579.9 1.3 fusion.80
  581.2 1.5 convolution_bitcast_fusion.3
  583.1 1.5 fusion.5
  584.6 39.6 %all-gather.32.cloned.1.call-done = f32[64,128,128]{2,1,0:T(8,128)} async-done(((f32[8,128,128]{2,1,0:T(8,128)}), f32[64,128,128]{2,1,0:T(8,128)}) %all-gather.32.cloned.1.call-update) | async-done | bytes 4194320 | tf_op jit(solution)/shard_map/all_gather | solution.py:13
  624.1 4.7 rev.7
  628.9 8.8 while.29
  628.9 1.2 fusion.136
  630.1 1.2 fusion.136
  631.4 1.2 fusion.136
  632.6 1.2 fusion.136
  633.8 1.2 fusion.136
  635.0 1.2 fusion.136
  636.2 1.2 fusion.136
  637.7 1.7 fusion.13
  642.5 2.9 convolution_dynamic-update-slice_fusion.6
  646.0 2.8 convolution_dynamic-update-slice_fusion.5
  648.8 3.0 convolution_dynamic-update-slice_fusion.4
  651.8 2.9 convolution_dynamic-update-slice_fusion.3
  654.6 2.8 convolution_dynamic-update-slice_fusion.2
  657.4 6.0 convolution_dynamic-update-slice_fusion.1
  663.4 6.0 convolution_dynamic-update-slice_fusion
  669.5 6.1 bitcast_dynamic-update-slice_fusion
  675.6 1.2 copy-done.4
  676.8 6.0 fusion.15
  688.8 1.3 fusion.20
  690.1 574.4 %reduce-scatter.2.cloned.1.call-done = f32[32,13568]{1,0:T(8,128)} async-done(((f32[1024,13568]{1,0:T(8,128)}), f32[32,13568]{1,0:T(8,128)}) %reduce-scatter.2.cloned.1.call-update) | async-done | bytes 1736720 | tf_op jit(solution)/shard_map/reduce_scatter | solution.py:210
  1264.5 2.0 fusion.72
  1266.5 2.2 slice_bitcast_fusion
  (192 shorter events, 34.9 us)
Async XLA Ops:
  7.2 63.0 %all-gather.18.cloned.1.call-start = ((), (), s32[]{:S(2)}) async-start(), calls=%async_computation.3 | async-start | bytes 2162688 | tf_op jit(solution)/shard_map/all_gather | solution.py:95
  7.9 120.6 %all-gather.16.cloned.1.call-start = ((), (), s32[]{:S(2)}) async-start(), calls=%async_computation.2 | async-start | bytes 2162688 | tf_op jit(solution)/shard_map/all_gather | solution.py:94
  8.7 178.3 %all-gather.14.cloned.1.call-start = ((), (), s32[]{:S(2)}) async-start(), calls=%async_computation.1 | async-start | bytes 2162688 | tf_op jit(solution)/shard_map/all_gather | solution.py:96
  9.4 235.7 %all-gather.20.cloned.1.call-start = ((), (), s32[]{:S(2)}) async-start(), calls=%async_computation.4 | async-start | bytes 2162688 | tf_op jit(solution)/shard_map/all_gather | solution.py:97
  10.0 282.7 %all-gather.30.cloned.1.call-start = ((), (), s32[]{:S(2)}) async-start(), calls=%async_computation.10 | async-start | bytes 4718592 | tf_op jit(solution)/shard_map/all_gather | solution.py:13
  14.0 56.3 %copy-start.54 = (f32[64]{0:T(128)}, f32[64]{0:T(128)S(1)}, u32[]{:S(2)}) copy-start(f32[64]{0:T(128)S(1)} %get-tuple-element.291) | copy-start | bytes 772
  72.7 1.1 copy-start.7
  73.8 54.8 %copy-start = (bf16[1,256,1024]{2,1,0:T(8,128)(2,1)S(1)}, bf16[1,256,1024]{2,1,0:T(8,128)(2,1)}, u32[]{:S(2)}) copy-start(bf16[1,256,1024]{2,1,0:T(8,128)(2,1)} %param.15) | copy-start | bytes 1572868
  130.9 1.0 copy-start.9
  133.3 1.3 copy-start.6
  135.3 56.0 %copy-start.27 = (bf16[256,8,128]{2,0,1:T(8,128)(2,1)}, bf16[256,8,128]{2,0,1:T(8,128)(2,1)S(1)}, u32[]{:S(2)}) copy-start(bf16[256,8,128]{2,0,1:T(8,128)(2,1)S(1)} %multiply_convert_fusion.9) | copy-start | bytes 1572868
  190.1 4.1 copy-start.55
  191.3 159.4 %all-gather.22.cloned.1.call-start = ((), (), s32[]{:S(2)}) async-start(), calls=%async_computation.5 | async-start | bytes 2162688 | tf_op jit(solution)/shard_map/all_gather | solution.py:98
  191.8 227.9 %all-gather.26.cloned.1.call-start = ((), (), s32[]{:S(2)}) async-start(), calls=%async_computation.7 | async-start | bytes 5947392 | tf_op jit(solution)/shard_map/all_gather | solution.py:100
  192.6 296.3 %all-gather.24.cloned.1.call-start = ((), (), s32[]{:S(2)}) async-start(), calls=%async_computation.6 | async-start | bytes 5947392 | tf_op jit(solution)/shard_map/all_gather | solution.py:99
  193.3 364.7 %all-gather.28.cloned.1.call-start = ((), (), s32[]{:S(2)}) async-start(), calls=%async_computation.8 | async-start | bytes 5947392 | tf_op jit(solution)/shard_map/all_gather | solution.py:101
  194.1 430.1 %all-gather.32.cloned.1.call-start = ((), (), s32[]{:S(2)}) async-start(), calls=%async_computation.11 | async-start | bytes 4718592 | tf_op jit(solution)/shard_map/all_gather | solution.py:13
  249.1 2.1 copy-start.52
  251.1 2.0 copy-start.46
  251.1 2.0 copy-start.48
  251.1 1.4 copy-start.51
  252.6 1.6 copy-start.32
  292.7 8.7 copy-start.34
  301.4 2.0 copy-start.16
  301.8 1.0 copy-start.1
  305.2 47.9 %copy-start.36 = (bf16[256,8,128]{0,2,1:T(8,128)(2,1)}, bf16[256,8,128]{0,2,1:T(8,128)(2,1)S(1)}, u32[]{:S(2)}) copy-start(bf16[256,8,128]{0,2,1:T(8,128)(2,1)S(1)} %get-tuple-element.295) | copy-start | bytes 1572868
  353.1 218.3 %copy-start.3 = (f32[256,1024]{1,0:T(8,128)}, f32[256,1024]{1,0:T(8,128)S(1)}, u32[]{:S(2)}) copy-start(f32[256,1024]{1,0:T(8,128)S(1)} %get-tuple-element.298) | copy-start | bytes 3145732
  353.2 135.6 %copy-start.22 = (bf16[256,1024]{1,0:T(8,128)(2,1)}, bf16[256,1024]{1,0:T(8,128)(2,1)S(1)}, u32[]{:S(2)}) copy-start(bf16[256,1024]{1,0:T(8,128)(2,1)S(1)} %multiply_convert_fusion.10) | copy-start | bytes 1572868
  425.6 132.5 %copy-start.24 = (bf16[1,256,1024]{2,1,0:T(8,128)(2,1)S(1)}, bf16[1,256,1024]{2,1,0:T(8,128)(2,1)}, u32[]{:S(2)}) copy-start(bf16[1,256,1024]{2,1,0:T(8,128)(2,1)} %param.25) | copy-start | bytes 1572868
  558.0 7.1 copy-start.53
  565.2 1.7 copy-start.20
  565.2 1.7 copy-start.18
  566.9 4.5 copy-start.25
  571.4 1.6 copy-start.14
  573.0 1.2 copy-start.2
  573.0 1.5 copy-start.45
  575.6 1.0 copy-start.35
  577.9 686.6 %reduce-scatter.2.cloned.1.call-start = ((), (), s32[]{:S(2)}) async-start(), calls=%async_computation.9 | async-start | bytes 57311232 | tf_op jit(solution)/shard_map/reduce_scatter | solution.py:210
  577.9 1.9 copy-start.44
  579.8 1.3 copy-start.49
  579.9 2.8 copy-start.47
  628.9 8.8 copy-start.28
  637.6 1.7 copy-start.33
  637.6 1.7 copy-start.42
  639.4 9.4 copy-start.40
  639.4 1.4 copy-start.11
  640.8 1.2 copy-start.10
  642.5 2.9 copy-start.8
  645.9 2.8 copy-start.29
  648.8 3.0 copy-start.38
  651.8 2.9 copy-start.37
  654.6 2.8 copy-start.21
  654.6 2.8 copy-start.23
  657.4 6.0 copy-start.19
  663.4 6.1 copy-start.17
  663.4 6.1 copy-start.26
  675.6 1.2 copy-start.4
  676.8 6.0 copy-start.13
  682.8 1.6 copy-start.15
  682.8 1.7 copy-start.30
  684.5 1.0 copy-start.41
  684.5 1.8 copy-start.50
  686.2 1.6 copy-start.12
  686.2 1.7 copy-start.39
  (3 other events, 2.8 us)
Sparse Core Ops, SparseCore 0:
  11.0 59.1 all-gather.17
  73.2 55.3 all-gather.15
  131.5 55.3 all-gather.13
  189.7 55.3 all-gather.19
  246.6 46.0 all-gather.29
  295.5 55.1 all-gather.21
  353.5 66.1 all-gather.25
  422.5 66.2 all-gather.23
  491.7 66.2 all-gather.27
  578.0 46.1 all-gather.31
  675.7 588.7 reduce-scatter.1
where the time goes:
time: 1280 us
  waiting for transfers between devices  1090 us (85%)
  matrix products  91.2 us (7%)
  other arithmetic  31.2 us (2%)
  local copies, waits for them, and re-layouts  29.8 us (2%)
  blocking collectives  15.6 us (1%)
  between operations  15.6 us (1%)
    reduce_scatter x1, waiting for transfers between devices, body(): lax.psum_scatter(jnp.concatenate([outer_sum(normed_low, grad_qpre), outer...  574 us
    all_gather x2, waiting for transfers between devices, entering(): pieces = jax.tree.map(lambda part: lax.all_gather(part, axis), value)  77.6 us
    all_gather x1, waiting for transfers between devices, body(): lax.all_gather(up_weight, ('items', 'seq'), axis=0, tiled=True)  66.4 us
    all_gather x1, waiting for transfers between devices, body(): lax.all_gather(down_weight, ('items', 'seq'), axis=1, tiled=True)  63.3 us
    all_gather x1, waiting for transfers between devices, body(): lax.all_gather(gate_weight, ('items', 'seq'), axis=0, tiled=True)  63.3 us
    all_gather x1, waiting for transfers between devices, body(): lax.all_gather(key_weight, ('items', 'seq'), axis=0, tiled=True)  55 us
    all_gather x1, waiting for transfers between devices, body(): lax.all_gather(query_weight, ('items', 'seq'), axis=0, tiled=True)  54.3 us
    all_gather x1, waiting for transfers between devices, body(): lax.all_gather(value_weight, ('items', 'seq'), axis=0, tiled=True)  51.6 us
  transfers between devices with their start and end apart: 11, of which 11 were waited for; matrix products, arithmetic and copies ran while one was open for 5% of the time, Pallas kernels for 0%

commit v1 on v0

v1 whole, which is shorter than its diff:
```python
import math

import jax
import jax.numpy as jnp
from jax import lax
from jax.sharding import PartitionSpec as P

epsilon = 1e-06
AXES = ("items", "seq")
f32 = jnp.float32
bf16 = jnp.bfloat16


def mm(a, b):
    return jnp.dot(a, b, preferred_element_type=f32)


def mm_tn(a, b):
    return lax.dot_general(a, b, (((0,), (0,)), ((), ())), preferred_element_type=f32)


def mm_nt(a, b):
    return lax.dot_general(a, b, (((1,), (1,)), ((), ())), preferred_element_type=f32)


def norm_factor(v):
    return lax.rsqrt(jnp.mean(v * v, axis=-1, keepdims=True) + epsilon)


def norm_back(normed, scale, grad):
    return scale * (grad - normed * jnp.mean(grad * normed, axis=-1, keepdims=True))


def pick(bit, a, b):
    return jnp.where(bit == 0, a, b)


def order(bit, own, other, axis):
    return jnp.where(
        bit == 0, jnp.concatenate([own, other], axis), jnp.concatenate([other, own], axis)
    )


class Place:
    def __init__(self, items, seqs):
        self.items, self.seqs, self.groups = items, seqs, seqs // 4
        self.count = items * seqs
        self.item = lax.axis_index("items")
        where = lax.axis_index("seq")
        self.core, self.pair, self.group = where % 2, (where // 2) % 2, where // 4
        self.member = where % 4

    def swap(self, v, mask):
        return lax.ppermute(v, AXES, [(d, d ^ mask) for d in range(self.count)])

    def core_swap(self, v):
        return self.swap(v, 1)

    def pair_swap(self, v):
        return self.swap(v, 2)

    def group_swap(self, v, k):
        return self.swap(v, 4 * k)

    def item_swap(self, v, k):
        return self.swap(v, self.seqs * k)

    def group_shift(self, v, k):
        pairs = []
        for d in range(self.count):
            g = (d % self.seqs) // 4 + k
            if 0 <= g < self.groups:
                pairs.append((d, d + 4 * k))
        return lax.ppermute(v, AXES, pairs)

    def spread(self, v):
        v = v[None]
        v = order(self.pair, v, self.pair_swap(v), 0)[:, None]
        return order(self.core, v, self.core_swap(v), 1)

    def collect(self, v):
        keep, send = pick(self.core, v[:, 0], v[:, 1]), pick(self.core, v[:, 1], v[:, 0])
        v = keep + self.core_swap(send.astype(bf16)).astype(f32)
        keep, send = pick(self.pair, v[0], v[1]), pick(self.pair, v[1], v[0])
        return keep + self.pair_swap(send.astype(bf16)).astype(f32)

    def exchange(self, v):
        keep, send = pick(self.core, v[:, 0], v[:, 1]), pick(self.core, v[:, 1], v[:, 0])
        v = order(self.core, keep[:, None], self.core_swap(send)[:, None], 1)
        keep, send = pick(self.pair, v[0], v[1]), pick(self.pair, v[1], v[0])
        return order(self.pair, keep[None], self.pair_swap(send)[None], 0)

    def permute(self, v):
        rows, width = v.shape
        block = width // (self.items * self.groups)
        v = v.reshape(rows, self.items, self.groups, block)
        for axis, size, here in ((1, self.items, self.item), (2, self.groups, self.group)):
            bit = 1
            while bit < size:
                shape = v.shape
                w = v.reshape(shape[:axis] + (size // (2 * bit), 2, bit) + shape[axis + 1 :])
                w = pick((here // bit) % 2, w, jnp.flip(w, axis + 1))
                v = w.reshape(shape)
                bit *= 2
        return v.reshape(rows, width)


def by_member(w, pad):
    rows, width = w.shape
    w = w.reshape(rows, 4, width // 4).transpose(1, 0, 2)
    return jnp.pad(w, ((0, 0), (0, 0), (0, pad))) if pad else w


def gather_weights(at, raw):
    v = raw.reshape((2, 2) + raw.shape[1:])
    v = at.exchange(v).reshape(-1, raw.shape[2])
    pieces = [v] + [at.group_swap(v, k) for k in range(1, at.groups)]
    half = max(1, at.groups // 2)
    table = {}
    for k, piece in enumerate(pieces):
        one, two = (1, 2) if k < half else (2, 1)
        first = at.item_swap(piece, one)
        second = at.item_swap(piece, two)
        table[0, k], table[one, k], table[two, k] = piece, first, second
        table[3, k] = at.item_swap(first, two)
    return jnp.concatenate(
        [table[i, k] for i in range(at.items) for k in range(at.groups)], axis=0
    )


def scatter_grads(at, grad):
    width = grad.shape[1]
    low = grad.reshape(at.items, at.groups, -1, width)
    half = max(1, at.groups // 2)
    sums = []
    for part, one, two in ((slice(0, half), 1, 2), (slice(half, at.groups), 2, 1)):
        v = low[:, part]
        if v.shape[1] == 0:
            continue
        got = at.item_swap(jnp.stack([v[one], v[3]]).astype(bf16), one).astype(f32)
        got2 = at.item_swap((v[two] + got[1]).astype(bf16), two).astype(f32)
        sums.append(v[0] + got[0] + got2)
    v = jnp.concatenate(sums, axis=0)
    total = v[0]
    for k in range(1, at.groups):
        total = total + at.group_swap(v[k].astype(bf16), k).astype(f32)
    total = total.reshape(2, 2, -1, width)
    keep, send = pick(at.pair, total[0], total[1]), pick(at.pair, total[1], total[0])
    got = at.pair_swap(send.astype(bf16)).astype(f32)
    v = order(at.pair, keep[None], got[None], 0)
    keep, send = pick(at.core, v[:, 0], v[:, 1]), pick(at.core, v[:, 1], v[:, 0])
    got = at.core_swap(send.astype(bf16)).astype(f32)
    v = order(at.core, keep[:, None], got[:, None], 1)
    return v.reshape(4, -1, width).transpose(1, 0, 2)


def rotation_tables(positions, head_size):
    half_width = head_size // 2
    pair_index = jnp.arange(half_width, dtype=jnp.int32)
    step_sizes = jnp.right_shift(jnp.full((half_width,), 8192, jnp.int32), pair_index // 5)
    phase_int = positions[:, None] * step_sizes[None, :] % 65536
    angles = phase_int.astype(f32) * (2.0 * math.pi / 65536.0)
    return (jnp.cos(angles), jnp.sin(angles))


def rotate(v, cosine, sine):
    half = v.shape[-1] // 2
    a, b = v[..., :half], v[..., half:]
    return jnp.concatenate([a * cosine - b * sine, a * sine + b * cosine], axis=-1)


def ein(spec, a, b):
    return jnp.einsum(spec, a, b, preferred_element_type=f32)


def make_body(items, seqs):
    def body(
        tokens,
        decay_rate,
        query_weight,
        key_weight,
        value_weight,
        update_weight,
        output_weight,
        gate_weight,
        up_weight,
        down_weight,
        cotangent,
    ):
        at = Place(items, seqs)
        width = tokens.shape[-1]
        rows = tokens.shape[1]
        heads = decay_rate.shape[0]
        size = width // heads
        own_heads = heads // 4
        own_width = width // 4
        hidden = gate_weight.shape[1] // 4
        pad = -hidden % 256
        wide = hidden + pad

        attn_raw = jnp.concatenate(
            [by_member(w, 0) for w in (query_weight, key_weight, value_weight, update_weight)], 2
        )
        ffn_raw = jnp.concatenate(
            [by_member(w, pad) for w in (gate_weight, up_weight, down_weight.T)]
            + [by_member(output_weight, 0)],
            2,
        )
        attn_w = gather_weights(at, attn_raw)
        ffn_w = gather_weights(at, ffn_raw)
        gate_w, up_w, down_w, out_part = (
            ffn_w[:, :wide],
            ffn_w[:, wide : 2 * wide],
            ffn_w[:, 2 * wide : 3 * wide],
            ffn_w[:, 3 * wide :],
        )
        out_w = at.spread(out_part).reshape(4, width, own_width).transpose(1, 0, 2)
        out_w = out_w.reshape(width, width)

        inputs = tokens.reshape(rows, width).astype(f32)
        scale_in = norm_factor(inputs)
        normed_in = inputs * scale_in
        h1 = at.spread(at.permute(normed_in.astype(bf16))).reshape(4 * rows, width)
        grad_ffn = cotangent.reshape(rows, width)
        cot = at.spread(at.permute(grad_ffn)).reshape(4 * rows, width)

        pre = mm(h1, attn_w).reshape(4, rows, 4, own_heads, size).transpose(2, 0, 3, 1, 4)
        query_pre, key_pre, update = pre[0], pre[1], pre[3]
        values = pre[2].astype(bf16)

        start = at.group * 4 * rows
        positions = start + jnp.arange(4 * rows, dtype=jnp.int32)
        cosine, sine = rotation_tables(positions, size)
        cosine, sine = (t.reshape(4, 1, rows, -1) for t in (cosine, sine))
        query_sig, key_sig = jax.nn.sigmoid(query_pre), jax.nn.sigmoid(key_pre)
        query_act = rotate(query_pre * query_sig, cosine, sine)
        key_act = rotate(key_pre * key_sig, cosine, sine)
        log_decay = lax.dynamic_slice(jnp.log(decay_rate), (at.member * own_heads,), (own_heads,))
        local = jnp.arange(rows).astype(f32)
        ld = log_decay[:, None]
        query_decay = jnp.exp(ld * (local + 1.0))[:, :, None]
        key_decay = jnp.exp(ld * (rows - 1.0 - local))[:, :, None]
        offset = local[:, None] - local[None, :]
        mask = jnp.where(
            offset >= 0.0, jnp.exp(log_decay[:, None, None] * jnp.maximum(offset, 0.0)), 0.0
        )
        queries, keys = query_act.astype(bf16), key_act.astype(bf16)
        query_scaled = (query_act * query_decay).astype(bf16)
        key_scaled = (key_act * key_decay).astype(bf16)
        factor = jnp.exp(log_decay * rows)[:, None, None]
        far = jnp.exp(log_decay * (4.0 * rows))[:, None, None]

        states = ein("bhse,bhsf->bhef", key_scaled, values)
        prefix = [jnp.zeros_like(states[0])]
        for b in range(4):
            prefix.append(factor * prefix[b] + states[b])
        before = jnp.zeros_like(states[0])
        weight = jnp.ones_like(far)
        for k in range(1, at.groups):
            before = before + weight * at.group_shift(prefix[4], k)
            weight = weight * far
        scores = ein("bhte,bhse->bhts", queries, keys)
        weight_low = (scores * mask).astype(bf16)
        intra = ein("bhts,bhse->bhte", weight_low, values)
        full = []
        weight = jnp.ones_like(factor)
        for b in range(4):
            full.append(prefix[b] + weight * before)
            weight = weight * factor
        prefix_low = jnp.stack(full).astype(bf16)
        attn = intra + ein("bhte,bhef->bhtf", query_scaled, prefix_low)
        scale_heads = norm_factor(attn)
        normed_heads = attn * scale_heads
        mixed_low = (normed_heads * update).astype(bf16)
        own = at.exchange(mixed_low.reshape((2, 2) + mixed_low.shape[1:]))
        own = own.reshape(heads, rows, size).transpose(1, 0, 2).reshape(rows, width)
        own = at.permute(own)
        resid = inputs + mm(own, out_w)
        scale_mid = norm_factor(resid)
        normed_mid = resid * scale_mid
        h2 = at.spread(at.permute(normed_mid.astype(bf16))).reshape(4 * rows, width)
        gate_act, up_act = mm(h2, gate_w), mm(h2, up_w)
        grad_hidden = mm(cot, down_w)
        hidden_low = (gate_act * up_act).astype(bf16)
        grad_gate = (grad_hidden * up_act).astype(bf16)
        grad_up = (grad_hidden * gate_act).astype(bf16)
        grad_mid = mm_nt(grad_gate, gate_w) + mm_nt(grad_up, up_w)
        grad_mid = at.permute(at.collect(grad_mid.reshape(2, 2, rows, width)))
        ffn_grads = jnp.concatenate(
            [mm_tn(h2, grad_gate), mm_tn(h2, grad_up), mm_tn(cot, hidden_low)], 1
        )
        ffn_own = scatter_grads(at, ffn_grads)
        ffn_out = at.permute(at.collect(mm_nt(hidden_low, down_w).reshape(2, 2, rows, width)))
        mixed = (resid + ffn_out).astype(bf16).reshape(tokens.shape)

        grad_resid = grad_ffn.astype(f32) + norm_back(normed_mid, scale_mid, grad_mid)
        grad_attn = grad_resid.astype(bf16)
        grad_mixed = at.permute(mm_nt(grad_attn, out_w).astype(bf16))
        grad_mixed = grad_mixed.reshape(rows, 2, 2, own_heads, size).transpose(1, 2, 3, 0, 4)
        keep = pick(at.pair, grad_mixed[0], grad_mixed[1])
        send = pick(at.pair, grad_mixed[1], grad_mixed[0])
        v = order(at.pair, keep[None], at.pair_swap(send)[None], 0)
        keep, send = pick(at.core, v[:, 0], v[:, 1]), pick(at.core, v[:, 1], v[:, 0])
        v = order(at.core, keep[:, None], at.core_swap(send)[:, None], 1)
        grad_mixed = v.reshape(4, own_heads, rows, size).astype(f32)
        out_grad = mm_tn(own, grad_attn).reshape(width, 2, 2, own_width).transpose(1, 2, 0, 3)
        out_grad = at.collect(out_grad)

        grad_update = (grad_mixed * normed_heads).astype(bf16)
        grad_raw = norm_back(normed_heads, scale_heads, grad_mixed * update).astype(bf16)
        grad_prefix = ein("bhte,bhtf->bhef", query_scaled, grad_raw)
        suffix = [jnp.zeros_like(before)]
        for b in range(4):
            suffix.append(factor * suffix[b] + grad_prefix[3 - b])
        after = jnp.zeros_like(before)
        weight = jnp.ones_like(far)
        for k in range(1, at.groups):
            after = after + weight * at.group_shift(suffix[4], -k)
            weight = weight * far
        grad_weight = ein("bhte,bhse->bhts", grad_raw, values)
        grad_scores = (grad_weight * mask).astype(bf16)
        grad_query = ein("bhts,bhse->bhte", grad_scores, keys)
        grad_key = ein("bhts,bhte->bhse", grad_scores, queries)
        grad_value = ein("bhts,bhte->bhse", weight_low, grad_raw)
        grad_qscaled = ein("bhtf,bhef->bhte", grad_raw, prefix_low)
        full = []
        weight = jnp.ones_like(factor)
        for b in range(4):
            full.append(suffix[b] + weight * after)
            weight = weight * factor
        state_low = jnp.stack(full[::-1]).astype(bf16)
        grad_kscaled = ein("bhsf,bhef->bhse", values, state_low)
        grad_value = (grad_value + ein("bhse,bhef->bhsf", key_scaled, state_low)).astype(bf16)
        grad_qact = grad_query + grad_qscaled * query_decay
        grad_kact = grad_key + grad_kscaled * key_decay
        grad_qpre = (
            rotate(grad_qact, cosine, -sine) * query_sig * (1.0 + query_pre * (1.0 - query_sig))
        ).astype(bf16)
        grad_kpre = (
            rotate(grad_kact, cosine, -sine) * key_sig * (1.0 + key_pre * (1.0 - key_sig))
        ).astype(bf16)
        grads = jnp.stack([grad_qpre, grad_kpre, grad_value, grad_update])
        grads = grads.transpose(1, 3, 0, 2, 4).reshape(4 * rows, 4 * own_width)
        attn_grads = jnp.concatenate([mm_tn(h1, grads), out_grad], 1)
        attn_own = scatter_grads(at, attn_grads)
        grad_in = at.permute(at.collect(mm_nt(grads, attn_w).reshape(2, 2, rows, width)))
        tokens_grad = (grad_resid + norm_back(normed_in, scale_in, grad_in)).reshape(tokens.shape)

        def owned(v, first, count):
            return v[:, :, first : first + count].reshape(v.shape[0], -1)

        return (
            mixed,
            tokens_grad,
            owned(attn_own, 0, own_width),
            owned(attn_own, own_width, own_width),
            owned(attn_own, 2 * own_width, own_width),
            owned(attn_own, 3 * own_width, own_width),
            owned(attn_own, 4 * own_width, own_width),
            owned(ffn_own, 0, hidden),
            owned(ffn_own, wide, hidden),
            owned(ffn_own, 2 * wide, hidden).T,
        )

    return body


def solution(mesh):
    act = P("items", "seq", None)
    row = P(("items", "seq"), None)
    col = P(None, ("items", "seq"))
    return jax.shard_map(
        make_body(mesh.shape["items"], mesh.shape["seq"]),
        mesh=mesh,
        in_specs=(act, P()) + (row,) * 7 + (col, act),
        out_specs=(act, act) + (row,) * 7 + (col,),
        check_vma=False,
    )
```

time: 1280 us -> 527 us (0.41)
  waiting for transfers between devices: 1090 us -> 150 us
  local copies, waits for them, and re-layouts: 29.8 us -> 146 us
  other arithmetic: 31.2 us -> 128 us
  starting transfers between devices: 0.43 us -> 49.3 us
  matrix products: 91.2 us -> 44.6 us
  blocking collectives: 15.6 us -> 0 us
    reduce_scatter x1 -> x0, waiting for transfers between devices: 574 us -> none  [body(): lax.psum_scatter(jnp.concatenate([outer_sum(normed_low, grad_qpre), outer...]
    all_gather x10 -> x0, waiting for transfers between devices: 511 us -> none  [the longest x2 77.6 us: entering(): pieces = jax.tree.map(lambda part: lax.all_gather(part, axis), value)]
    ppermute x0 -> x54, waiting for transfers between devices: none -> 150 us  [the longest x52 122 us: swap(): return lax.ppermute(v, AXES, [(d, d ^ mask) for d in range(self.count)])]
    ppermute x0 -> x54, starting transfers between devices: none -> 49.3 us  [the longest x52 46 us: swap(): return lax.ppermute(v, AXES, [(d, d ^ mask) for d in range(self.count)])]
    dot_general x36 -> x27, matrix products: 91.2 us -> 44.6 us  [the longest x5 17.5 us: mm_tn(): lax.dot_general(a, b, (((0,), (0,)), ((), ())), preferred_element_type=f32)]
    rev x2 -> x8, local copies, waits for them, and re-layouts: 4.72 us -> 36.2 us  [permute(): w = pick(here // bit % 2, w, jnp.flip(w, axis + 1))]
    another operation x0 -> x16, local copies, waits for them, and re-layouts: none -> 28.3 us  [the longest x5 12.6 us: permute(): return v.reshape(rows, width)]
    reshape x0 -> x19, local copies, waits for them, and re-layouts: none -> 27.7 us  [the longest x2 15.9 us: scatter_grads(): low = grad.reshape(at.items, at.groups, -1, width)]
  transfers between devices with their start and end apart: 11 -> 54, of which waited for: 11 -> 25; matrix products, arithmetic and copies ran while one was open for 5% -> 50% of each run, Pallas kernels for 0% -> 0%
where the time goes in v1:
time: 527 us; the launch traced here: 521 us
  waiting for transfers between devices  150 us (28%)
  local copies, waits for them, and re-layouts  146 us (28%)
  other arithmetic  128 us (24%)
  starting transfers between devices  49.3 us (9%)
  matrix products  44.6 us (8%)
    ppermute x52, waiting for transfers between devices, swap(): return lax.ppermute(v, AXES, [(d, d ^ mask) for d in range(self.count)])  122 us
    ppermute x52, starting transfers between devices, swap(): return lax.ppermute(v, AXES, [(d, d ^ mask) for d in range(self.count)])  46 us
    rev x8, local copies, waits for them, and re-layouts, permute(): w = pick(here // bit % 2, w, jnp.flip(w, axis + 1))  36.2 us
    ppermute x2, waiting for transfers between devices, group_shift(): return lax.ppermute(v, AXES, pairs)  27.3 us
    unnamed x157, local copies, waits for them, and re-layouts  25.9 us
    select_n x20, other arithmetic, order(): jnp.where(bit == 0, jnp.concatenate([own, other], axis), jnp.concatenate(...  21.1 us
    dot_general x5, matrix products, mm_tn(): lax.dot_general(a, b, (((0,), (0,)), ((), ())), preferred_element_type=f32)  17.5 us
    select_n x32, other arithmetic, pick(): return jnp.where(bit == 0, a, b)  15.9 us
  transfers between devices with their start and end apart: 54, of which 25 were waited for; matrix products, arithmetic and copies ran while one was open for 50% of the time, Pallas kernels for 0%

profile of v1, /device:TPU:0, one launch (start us, length us, event | category | flops | bytes accessed | tf_op | source)
XLA Modules:
  0.0 520.5 jit_solution(8573612800656337474)
XLA Ops:
  5.7 3.0 rev.80
  10.0 3.0 collective-permute-start
  18.3 4.0 rev.92
  25.8 5.4 %collective-permute-done.3 = bf16[2,32,1024]{2,1,0:T(8,128)(2,1)S(1)} collective-permute-done((bf16[2,32,1024]{2,1,0:T(8,128)(2,1)S(1)}, bf16[2,32,1024]{2,1,0:T(8,128)(2,1)S(1)}, u32[]{:S(2)}, u32[]{:S(2)}) %collective-permute-start.3) | collective-permute-done | bytes 131104 | tf_op jit(solution)/shard_map/ppermute | solution.py:54
  31.2 2.7 collective-permute-start.4
  39.3 5.9 %collective-permute-done.4 = bf16[128,1024]{1,0:T(8,128)(2,1)S(1)} collective-permute-done((bf16[128,1024]{1,0:T(8,128)(2,1)S(1)}, bf16[128,1024]{1,0:T(8,128)(2,1)S(1)}, u32[]{:S(2)}, u32[]{:S(2)}) %collective-permute-start.4) | collective-permute-done | bytes 262176 | tf_op jit(solution)/shard_map/ppermute | solution.py:54
  60.1 3.3 collective-permute-done.9
  64.4 11.2 %collective-permute-done.10 = bf16[128,1024]{1,0:T(8,128)(2,1)S(1)} collective-permute-done((bf16[128,1024]{1,0:T(8,128)(2,1)S(1)}, bf16[128,1024]{1,0:T(8,128)(2,1)S(1)}, u32[]{:S(2)}, u32[]{:S(2)}) %collective-permute-start.10) | collective-permute-done | bytes 262176 | tf_op jit(solution)/shard_map/ppermute | solution.py:54
  76.3 4.0 copy.238
  80.3 3.7 collective-permute-done.16
  92.2 2.4 convolution_bitcast_fusion.1
  107.7 7.3 %collective-permute-done.21 = bf16[128,2560]{1,0:T(8,128)(2,1)S(1)} collective-permute-done((bf16[128,2560]{1,0:T(8,128)(2,1)}, bf16[128,2560]{1,0:T(8,128)(2,1)S(1)}, u32[]{:S(2)}, u32[]{:S(2)}) %collective-permute-start.21) | collective-permute-done | bytes 655392 | tf_op jit(solution)/shard_map/ppermute | solution.py:54
  115.8 3.2 collective-permute-done.22
  121.0 3.5 collective-permute-start.23
  125.4 11.8 %collective-permute-done.23 = bf16[1,1024,256]{2,1,0:T(8,128)(2,1)S(1)} collective-permute-done((bf16[1,1024,256]{2,1,0:T(8,128)(2,1)S(1)}, bf16[1,1024,256]{2,1,0:T(8,128)(2,1)S(1)}, u32[]{:S(2)}, u32[]{:S(2)}) %collective-permute-start.23) | collective-permute-done | bytes 524320 | tf_op jit(solution)/shard_map/ppermute | solution.py:54
  146.6 4.0 rev.83
  151.8 3.2 maximum_select_fusion.1
  155.0 3.0 copy.253
  167.3 5.8 %rev.86 = bf16[256,4,1,2,1,128]{5,3,1,0,4,2:T(2,128)(2,1)} reverse(bf16[256,4,1,2,1,128]{5,3,1,0,4,2:T(2,128)(2,1)} %bitcast.627), dimensions={3} | reverse | bytes 1048576 | tf_op jit(solution)/shard_map/jit(_flip)/rev | solution.py:102
  181.2 2.7 maximum_select_fusion.9
  186.1 4.4 collective-permute-done.25
  190.4 2.7 maximum_select_fusion.8
  193.1 3.1 reshape.1077
  196.2 3.9 maximum_select_fusion.3
  202.3 2.8 maximum_select_fusion.2
  205.2 3.3 fusion.10
  214.1 3.5 fusion.160
  219.6 3.5 fusion.159
  223.2 3.6 fusion.158
  231.8 9.2 %pad_maximum_fusion = f32[1024,2304]{0,1:T(8,128)} fusion(f32[1024,768]{0,1:T(8,128)} %fusion.160, f32[1024,768]{0,1:T(8,128)} %fusion.159, f32[1024,768]{0,1:T(8,128)} %fusion.158), kind=kLoop, calls=%fused_computation | loop fusion | flops 4718592 | bytes 18874368 | tf_op jit(solution)/shard_map/concatenate | solution.py:289
  241.0 10.0 %copy.319 = f32[1024,2304]{1,0:T(8,128)} copy(f32[1024,2304]{0,1:T(8,128)} %pad_maximum_fusion) | data formatting | bytes 18874368 | tf_op jit(solution)/shard_map/reshape | solution.py:133
  251.0 4.2 convert.68
  264.9 19.1 %collective-permute-done.47 = bf16[2,1,128,2304]{3,2,1,0:T(8,128)(2,1)S(1)} collective-permute-done((bf16[2,1,128,2304]{3,2,1,0:T(8,128)(2,1)S(1)}, bf16[2,1,128,2304]{3,2,1,0:T(8,128)(2,1)S(1)}, u32[]{:S(2)}, u32[]{:S(2)}) %collective-permute-start.47) | collective-permute-done | bytes 1179680 | tf_op jit(solution)/shard_map/ppermute | solution.py:54
  285.0 3.8 fusion.79
  292.0 3.1 reshape_reshape.90
  298.8 6.1 %rev.95 = f32[256,4,1,2,1,128]{5,3,1,0,4,2:T(2,128)} reverse(f32[256,4,1,2,1,128]{5,3,1,0,4,2:T(2,128)} %bitcast.595), dimensions={3} | reverse | bytes 2097152 | tf_op jit(solution)/shard_map/jit(_flip)/rev | solution.py:102
  304.9 2.3 broadcast_select_fusion.12
  307.2 3.1 reshape_reshape.93
  315.0 3.1 reshape_reshape.84
  321.7 6.2 %rev.89 = f32[256,4,1,2,1,128]{5,3,1,0,4,2:T(2,128)} reverse(f32[256,4,1,2,1,128]{5,3,1,0,4,2:T(2,128)} %bitcast.597), dimensions={3} | reverse | bytes 2097152 | tf_op jit(solution)/shard_map/jit(_flip)/rev | solution.py:102
  327.9 2.3 broadcast_select_fusion.14
  330.3 3.0 reshape_reshape.87
  333.3 3.3 convert_bitcast_fusion
  341.6 2.7 rev.98
  349.8 2.7 collective-permute-done.33
  352.8 2.6 fusion.80
  355.4 4.4 collective-permute-start.51
  365.8 26.3 %collective-permute-done.35 = f32[2,128,128]{2,1,0:T(8,128)S(1)} collective-permute-done((f32[2,128,128]{2,1,0:T(8,128)S(1)}, f32[2,128,128]{2,1,0:T(8,128)S(1)}, u32[]{:S(2)}, u32[]{:S(2)}) %collective-permute-start.35) | collective-permute-done | bytes 131104 | tf_op jit(solution)/shard_map/ppermute | solution.py:74
  395.2 4.0 fusion.2
  402.4 4.2 copy.279
  406.5 4.6 reshape.1062
  411.2 6.1 %fusion.157 = f32[1024,1024]{0,1:T(8,128)} fusion(bf16[1024,1024]{1,0:T(8,128)(2,1)S(1)} %bitcast.642, bf16[1024,1024]{1,0:T(8,128)(2,1)} %reshape.1062), kind=kOutput, calls=%fused_computation.378 | convolution fusion | flops 2147483648 | bytes 8388608 | tf_op jit(solution)/shard_map/dot_general | solution.py:19
  424.3 4.9 collective-permute-done.52
  435.1 4.9 collective-permute-done.39
  441.3 5.3 %pad_maximum_fusion.1 = f32[1024,1280]{0,1:T(8,128)} fusion(f32[1024,256]{0,1:T(8,128)S(1)} %bitcast_add_fusion.3, f32[1024,1024]{0,1:T(8,128)} %fusion.157), kind=kLoop, calls=%fused_computation.1 | loop fusion | flops 1310720 | bytes 10485760 | tf_op jit(solution)/shard_map/concatenate | solution.py:344
  446.6 5.9 %copy.318 = f32[1024,1280]{1,0:T(8,128)} copy(f32[1024,1280]{0,1:T(8,128)} %pad_maximum_fusion.1) | data formatting | bytes 10485760 | tf_op jit(solution)/shard_map/reshape | solution.py:133
  452.5 2.9 convert.67
  460.7 10.9 %collective-permute-done.37 = bf16[256,1024]{1,0:T(8,128)(2,1)S(1)} collective-permute-done((bf16[256,1024]{1,0:T(8,128)(2,1)S(1)}, bf16[256,1024]{1,0:T(8,128)(2,1)S(1)}, u32[]{:S(2)}, u32[]{:S(2)}) %collective-permute-start.37) | collective-permute-done | bytes 524320 | tf_op jit(solution)/shard_map/ppermute | solution.py:54
  473.9 4.4 rev.101
  484.3 4.4 multiply_reduce_fusion
  492.6 3.1 reshape_reshape.100
  495.8 2.5 fusion.64
  498.3 10.0 %collective-permute-done.44 = bf16[128,1280]{1,0:T(8,128)(2,1)} collective-permute-done((bf16[128,1280]{1,0:T(8,128)(2,1)}, bf16[128,1280]{1,0:T(8,128)(2,1)}, u32[]{:S(2)}, u32[]{:S(2)}) %collective-permute-start.44) | collective-permute-done | bytes 327712 | tf_op jit(solution)/shard_map/ppermute | solution.py:54
  509.7 5.5 %collective-permute-done.45 = bf16[2,32,1280]{2,1,0:T(8,128)(2,1)S(1)} collective-permute-done((bf16[2,32,1280]{2,1,0:T(8,128)(2,1)S(1)}, bf16[2,32,1280]{2,1,0:T(8,128)(2,1)S(1)}, u32[]{:S(2)}, u32[]{:S(2)}) %collective-permute-start.45) | collective-permute-done | bytes 163872 | tf_op jit(solution)/shard_map/ppermute | solution.py:54
  (434 shorter events, 192.4 us)
Async XLA Ops:
  5.7 7.5 %copy-start.55 = (bf16[32,1024]{1,0:T(8,128)(2,1)S(1)}, bf16[32,1024]{1,0:T(8,128)(2,1)}, u32[]{:S(2)}) copy-start(bf16[32,1024]{1,0:T(8,128)(2,1)} %param.13) | copy-start | bytes 196612
  10.0 39.6 %collective-permute-start = (bf16[1,256,1024]{2,1,0:T(8,128)(2,1)}, bf16[1,256,1024]{2,1,0:T(8,128)(2,1)}, u32[]{:S(2)}, u32[]{:S(2)}) collective-permute-start(bf16[1,256,1024]{2,1,0:T(8,128)(2,1)} %broadcast_in_dim_reshape_reshape.9), channel_id=1, source_target_pairs={{0,2},{1,3},{2,0},{3,1},{4,6},{5,7},{6,4},{7,5},{8,10},{9,11},{10,... | collective-permute-start | bytes 1572872 | tf_op jit(solution)/shard_map/ppermute | solution.py:54
  13.5 12.2 %collective-permute-start.2 = (bf16[2,32,1024]{2,1,0:T(8,128)(2,1)S(1)}, bf16[2,32,1024]{2,1,0:T(8,128)(2,1)S(1)}, u32[]{:S(2)}, u32[]{:S(2)}) collective-permute-start(bf16[2,32,1024]{2,1,0:T(8,128)(2,1)S(1)} %fusion.105), channel_id=1, source_target_pairs={{0,1},{1,0},{2,3},{3,2},{4,5},{5,4},{6,7},{7,6},{8,9},{9,8},{10,11... | collective-permute-start | bytes 393224 | tf_op jit(solution)/shard_map/ppermute | solution.py:54
  15.6 22.0 %collective-permute-start.14 = (bf16[2,32,2560]{2,1,0:T(8,128)(2,1)}, bf16[2,32,2560]{2,1,0:T(8,128)(2,1)}, u32[]{:S(2)}, u32[]{:S(2)}) collective-permute-start(bf16[2,32,2560]{2,1,0:T(8,128)(2,1)} %get-tuple-element.63), channel_id=1, source_target_pairs={{0,1},{1,0},{2,3},{3,2},{4,5},{5,4},{6,7},{7,6},{8,9},{9,8},{10,11... | collective-permute-start | bytes 983048 | tf_op jit(solution)/shard_map/ppermute | solution.py:54
  24.9 73.7 %copy-start.31 = (f32[2,256,256]{2,1,0:T(8,128)}, f32[2,256,256]{2,1,0:T(8,128)S(1)}, u32[]{:S(2)}) copy-start(f32[2,256,256]{2,1,0:T(8,128)S(1)} %exponential_select_fusion) | copy-start | bytes 1572868
  25.6 75.0 %copy-start.60 = (f32[2]{0:T(128)}, f32[2]{0:T(128)S(1)}, u32[]{:S(2)}) copy-start(f32[2]{0:T(128)S(1)} %get-tuple-element.80) | copy-start | bytes 28
  25.6 75.0 %copy-start.62 = (f32[2]{0:T(128)}, f32[2]{0:T(128)S(1)}, u32[]{:S(2)}) copy-start(f32[2]{0:T(128)S(1)} %get-tuple-element.81) | copy-start | bytes 28
  25.7 5.5 %collective-permute-start.3 = (bf16[2,32,1024]{2,1,0:T(8,128)(2,1)S(1)}, bf16[2,32,1024]{2,1,0:T(8,128)(2,1)S(1)}, u32[]{:S(2)}, u32[]{:S(2)}) collective-permute-start(bf16[2,32,1024]{2,1,0:T(8,128)(2,1)S(1)} %fusion.106), channel_id=1, source_target_pairs={{0,2},{1,3},{2,0},{3,1},{4,6},{5,7},{6,4},{7,5},{8,10},{9,11},{10,... | collective-permute-start | bytes 393224 | tf_op jit(solution)/shard_map/ppermute | solution.py:54
  31.2 14.1 %collective-permute-start.4 = (bf16[128,1024]{1,0:T(8,128)(2,1)S(1)}, bf16[128,1024]{1,0:T(8,128)(2,1)S(1)}, u32[]{:S(2)}, u32[]{:S(2)}) collective-permute-start(bf16[128,1024]{1,0:T(8,128)(2,1)S(1)} %bitcast.660), channel_id=1, source_target_pairs={{0,4},{1,5},{2,6},{3,7},{4,0},{5,1},{6,2},{7,3},{8,12},{9,13},{10,... | collective-permute-start | bytes 786440 | tf_op jit(solution)/shard_map/ppermute | solution.py:54
  33.8 13.5 %collective-permute-start.5 = (bf16[128,1024]{1,0:T(8,128)(2,1)S(1)}, bf16[128,1024]{1,0:T(8,128)(2,1)S(1)}, u32[]{:S(2)}, u32[]{:S(2)}) collective-permute-start(bf16[128,1024]{1,0:T(8,128)(2,1)S(1)} %bitcast.661), channel_id=1, source_target_pairs={{0,8},{1,9},{2,10},{3,11},{4,12},{5,13},{6,14},{7,15},{8,0},{9,1},... | collective-permute-start | bytes 786440 | tf_op jit(solution)/shard_map/ppermute | solution.py:54
  35.3 21.7 %collective-permute-start.7 = (bf16[128,1024]{1,0:T(8,128)(2,1)S(1)}, bf16[128,1024]{1,0:T(8,128)(2,1)S(1)}, u32[]{:S(2)}, u32[]{:S(2)}) collective-permute-start(bf16[128,1024]{1,0:T(8,128)(2,1)S(1)} %bitcast.662), channel_id=1, source_target_pairs={{0,16},{1,17},{2,18},{3,19},{4,20},{5,21},{6,22},{7,23},{8,24},{9,... | collective-permute-start | bytes 786440 | tf_op jit(solution)/shard_map/ppermute | solution.py:54
  38.8 13.4 %collective-permute-start.15 = (bf16[2,32,2560]{2,1,0:T(8,128)(2,1)S(1)}, bf16[2,32,2560]{2,1,0:T(8,128)(2,1)S(1)}, u32[]{:S(2)}, u32[]{:S(2)}) collective-permute-start(bf16[2,32,2560]{2,1,0:T(8,128)(2,1)S(1)} %get-tuple-element.61), channel_id=1, source_target_pairs={{0,2},{1,3},{2,0},{3,1},{4,6},{5,7},{6,4},{7,5},{8,10},{9,11},{10,... | collective-permute-start | bytes 983048 | tf_op jit(solution)/shard_map/ppermute | solution.py:54
  45.3 10.6 %collective-permute-start.6 = (bf16[128,1024]{1,0:T(8,128)(2,1)S(1)}, bf16[128,1024]{1,0:T(8,128)(2,1)S(1)}, u32[]{:S(2)}, u32[]{:S(2)}) collective-permute-start(bf16[128,1024]{1,0:T(8,128)(2,1)S(1)} %collective-permute-done.4), channel_id=1, source_target_pairs={{0,8},{1,9},{2,10},{3,11},{4,12},{5,13},{6,14},{7,15},{8,0},{9,1},... | collective-permute-start | bytes 786440 | tf_op jit(solution)/shard_map/ppermute | solution.py:54
  47.4 9.7 %collective-permute-start.8 = (bf16[128,1024]{1,0:T(8,128)(2,1)S(1)}, bf16[128,1024]{1,0:T(8,128)(2,1)S(1)}, u32[]{:S(2)}, u32[]{:S(2)}) collective-permute-start(bf16[128,1024]{1,0:T(8,128)(2,1)S(1)} %collective-permute-done.4), channel_id=1, source_target_pairs={{0,16},{1,17},{2,18},{3,19},{4,20},{5,21},{6,22},{7,23},{8,24},{9,... | collective-permute-start | bytes 786440 | tf_op jit(solution)/shard_map/ppermute | solution.py:54
  53.1 30.9 %collective-permute-start.16 = (bf16[128,2560]{1,0:T(8,128)(2,1)}, bf16[128,2560]{1,0:T(8,128)(2,1)}, u32[]{:S(2)}, u32[]{:S(2)}) collective-permute-start(bf16[128,2560]{1,0:T(8,128)(2,1)} %bitcast.62), channel_id=1, source_target_pairs={{0,4},{1,5},{2,6},{3,7},{4,0},{5,1},{6,2},{7,3},{8,12},{9,13},{10,... | collective-permute-start | bytes 1966088 | tf_op jit(solution)/shard_map/ppermute | solution.py:54
  53.1 30.9 %collective-permute-start.17 = (bf16[128,2560]{1,0:T(8,128)(2,1)}, bf16[128,2560]{1,0:T(8,128)(2,1)}, u32[]{:S(2)}, u32[]{:S(2)}) collective-permute-start(bf16[128,2560]{1,0:T(8,128)(2,1)} %bitcast.62), channel_id=1, source_target_pairs={{0,8},{1,9},{2,10},{3,11},{4,12},{5,13},{6,14},{7,15},{8,0},{9,1},... | collective-permute-start | bytes 1966088 | tf_op jit(solution)/shard_map/ppermute | solution.py:54
  55.8 7.6 %collective-permute-start.9 = (bf16[128,1024]{1,0:T(8,128)(2,1)S(1)}, bf16[128,1024]{1,0:T(8,128)(2,1)S(1)}, u32[]{:S(2)}, u32[]{:S(2)}) collective-permute-start(bf16[128,1024]{1,0:T(8,128)(2,1)S(1)} %collective-permute-done.5), channel_id=1, source_target_pairs={{0,16},{1,17},{2,18},{3,19},{4,20},{5,21},{6,22},{7,23},{8,24},{9,... | collective-permute-start | bytes 786440 | tf_op jit(solution)/shard_map/ppermute | solution.py:54
  57.0 33.0 %collective-permute-start.1 = (bf16[2,1,256,1024]{3,2,1,0:T(8,128)(2,1)S(1)}, bf16[2,1,256,1024]{3,2,1,0:T(8,128)(2,1)S(1)}, u32[]{:S(2)}, u32[]{:S(2)}) collective-permute-start(bf16[2,1,256,1024]{3,2,1,0:T(8,128)(2,1)S(1)} %maximum_select_fusion.6), channel_id=1, source_target_pairs={{0,1},{1,0},{2,3},{3,2},{4,5},{5,4},{6,7},{7,6},{8,9},{9,8},{10,11... | collective-permute-start | bytes 3145736 | tf_op jit(solution)/shard_map/ppermute | solution.py:54
  57.0 18.6 %collective-permute-start.10 = (bf16[128,1024]{1,0:T(8,128)(2,1)S(1)}, bf16[128,1024]{1,0:T(8,128)(2,1)S(1)}, u32[]{:S(2)}, u32[]{:S(2)}) collective-permute-start(bf16[128,1024]{1,0:T(8,128)(2,1)S(1)} %collective-permute-done.8), channel_id=1, source_target_pairs={{0,8},{1,9},{2,10},{3,11},{4,12},{5,13},{6,14},{7,15},{8,0},{9,1},... | collective-permute-start | bytes 786440 | tf_op jit(solution)/shard_map/ppermute | solution.py:54
  63.4 41.4 %collective-permute-start.19 = (bf16[128,2560]{1,0:T(8,128)(2,1)}, bf16[128,2560]{1,0:T(8,128)(2,1)}, u32[]{:S(2)}, u32[]{:S(2)}) collective-permute-start(bf16[128,2560]{1,0:T(8,128)(2,1)} %bitcast.62), channel_id=1, source_target_pairs={{0,16},{1,17},{2,18},{3,19},{4,20},{5,21},{6,22},{7,23},{8,24},{9,... | collective-permute-start | bytes 1966088 | tf_op jit(solution)/shard_map/ppermute | solution.py:54
  84.0 19.9 %collective-permute-start.18 = (bf16[128,2560]{1,0:T(8,128)(2,1)}, bf16[128,2560]{1,0:T(8,128)(2,1)S(1)}, u32[]{:S(2)}, u32[]{:S(2)}) collective-permute-start(bf16[128,2560]{1,0:T(8,128)(2,1)} %collective-permute-done.16), channel_id=1, source_target_pairs={{0,8},{1,9},{2,10},{3,11},{4,12},{5,13},{6,14},{7,15},{8,0},{9,1},... | collective-permute-start | bytes 1966088 | tf_op jit(solution)/shard_map/ppermute | solution.py:54
  84.0 17.8 %collective-permute-start.20 = (bf16[128,2560]{1,0:T(8,128)(2,1)}, bf16[128,2560]{1,0:T(8,128)(2,1)S(1)}, u32[]{:S(2)}, u32[]{:S(2)}) collective-permute-start(bf16[128,2560]{1,0:T(8,128)(2,1)} %collective-permute-done.16), channel_id=1, source_target_pairs={{0,16},{1,17},{2,18},{3,19},{4,20},{5,21},{6,22},{7,23},{8,24},{9,... | collective-permute-start | bytes 1966088 | tf_op jit(solution)/shard_map/ppermute | solution.py:54
  84.0 30.9 %collective-permute-start.21 = (bf16[128,2560]{1,0:T(8,128)(2,1)}, bf16[128,2560]{1,0:T(8,128)(2,1)S(1)}, u32[]{:S(2)}, u32[]{:S(2)}) collective-permute-start(bf16[128,2560]{1,0:T(8,128)(2,1)} %collective-permute-done.17), channel_id=1, source_target_pairs={{0,16},{1,17},{2,18},{3,19},{4,20},{5,21},{6,22},{7,23},{8,24},{9,... | collective-permute-start | bytes 1966088 | tf_op jit(solution)/shard_map/ppermute | solution.py:54
  96.6 4.0 collective-permute-start.11
  101.5 23.0 %collective-permute-start.12 = (bf16[2,2,256,128]{2,3,1,0:T(8,128)(2,1)S(1)}, bf16[2,2,256,128]{2,3,1,0:T(8,128)(2,1)S(1)}, u32[]{:S(2)}, u32[]{:S(2)}) collective-permute-start(bf16[2,2,256,128]{2,3,1,0:T(8,128)(2,1)S(1)} %fusion.102), channel_id=1, source_target_pairs={{0,1},{1,0},{2,3},{3,2},{4,5},{5,4},{6,7},{7,6},{8,9},{9,8},{10,11... | collective-permute-start | bytes 786440 | tf_op jit(solution)/shard_map/ppermute | solution.py:54
  101.8 17.2 %collective-permute-start.22 = (bf16[128,2560]{1,0:T(8,128)(2,1)S(1)}, bf16[128,2560]{1,0:T(8,128)(2,1)S(1)}, u32[]{:S(2)}, u32[]{:S(2)}) collective-permute-start(bf16[128,2560]{1,0:T(8,128)(2,1)S(1)} %collective-permute-done.20), channel_id=1, source_target_pairs={{0,8},{1,9},{2,10},{3,11},{4,12},{5,13},{6,14},{7,15},{8,0},{9,1},... | collective-permute-start | bytes 1966088 | tf_op jit(solution)/shard_map/ppermute | solution.py:54
  121.0 16.3 %collective-permute-start.23 = (bf16[1,1024,256]{2,1,0:T(8,128)(2,1)S(1)}, bf16[1,1024,256]{2,1,0:T(8,128)(2,1)S(1)}, u32[]{:S(2)}, u32[]{:S(2)}) collective-permute-start(bf16[1,1024,256]{2,1,0:T(8,128)(2,1)S(1)} %get-tuple-element.25), channel_id=1, source_target_pairs={{0,2},{1,3},{2,0},{3,1},{4,6},{5,7},{6,4},{7,5},{8,10},{9,11},{10,... | collective-permute-start | bytes 1572872 | tf_op jit(solution)/shard_map/ppermute | solution.py:54
  124.5 13.0 %copy-start.41 = (bf16[256,4,1,2,1,128]{5,3,1,0,4,2:T(2,128)(2,1)S(1)}, bf16[256,4,1,2,1,128]{5,3,1,0,4,2:T(2,128)(2,1)}, u32[]{:S(2)}) copy-start(bf16[256,4,1,2,1,128]{5,3,1,0,4,2:T(2,128)(2,1)} %rev.92) | copy-start | bytes 1572868
  125.4 16.5 %collective-permute-start.13 = (bf16[2,2,256,128]{2,3,1,0:T(8,128)(2,1)}, bf16[2,2,256,128]{2,3,1,0:T(8,128)(2,1)}, u32[]{:S(2)}, u32[]{:S(2)}) collective-permute-start(bf16[2,2,256,128]{2,3,1,0:T(8,128)(2,1)} %get-tuple-element.67), channel_id=1, source_target_pairs={{0,2},{1,3},{2,0},{3,1},{4,6},{5,7},{6,4},{7,5},{8,10},{9,11},{10,... | collective-permute-start | bytes 786440 | tf_op jit(solution)/shard_map/ppermute | solution.py:54
  137.4 14.4 %collective-permute-start.24 = (bf16[2,1,1024,256]{3,2,1,0:T(8,128)(2,1)S(1)}, bf16[2,1,1024,256]{3,2,1,0:T(8,128)(2,1)}, u32[]{:S(2)}, u32[]{:S(2)}) collective-permute-start(bf16[2,1,1024,256]{3,2,1,0:T(8,128)(2,1)S(1)} %maximum_select_fusion.7), channel_id=1, source_target_pairs={{0,1},{1,0},{2,3},{3,2},{4,5},{5,4},{6,7},{7,6},{8,9},{9,8},{10,11... | collective-permute-start | bytes 3145736 | tf_op jit(solution)/shard_map/ppermute | solution.py:54
  137.6 8.5 %copy-start.34 = (bf16[256,1,1,8,1,128]{5,3,1,0,4,2:T(8,128)(2,1)}, bf16[256,1,1,8,1,128]{5,3,1,0,4,2:T(8,128)(2,1)S(1)}, u32[]{:S(2)}) copy-start(bf16[256,1,1,8,1,128]{5,3,1,0,4,2:T(8,128)(2,1)S(1)} %broadcast_select_fusion.13) | copy-start | bytes 1572868
  138.8 42.4 %collective-permute-start.29 = (bf16[1,256,1024]{2,1,0:T(8,128)(2,1)}, bf16[1,256,1024]{2,1,0:T(8,128)(2,1)}, u32[]{:S(2)}, u32[]{:S(2)}) collective-permute-start(bf16[1,256,1024]{2,1,0:T(8,128)(2,1)} %broadcast_in_dim_reshape_reshape.11), channel_id=1, source_target_pairs={{0,2},{1,3},{2,0},{3,1},{4,6},{5,7},{6,4},{7,5},{8,10},{9,11},{10,... | collective-permute-start | bytes 1572872 | tf_op jit(solution)/shard_map/ppermute | solution.py:54
  177.2 13.3 %collective-permute-start.25 = (bf16[1,256,1024]{2,1,0:T(8,128)(2,1)}, bf16[1,256,1024]{2,1,0:T(8,128)(2,1)}, u32[]{:S(2)}, u32[]{:S(2)}) collective-permute-start(bf16[1,256,1024]{2,1,0:T(8,128)(2,1)} %broadcast_in_dim_reshape_reshape.10), channel_id=1, source_target_pairs={{0,2},{1,3},{2,0},{3,1},{4,6},{5,7},{6,4},{7,5},{8,10},{9,11},{10,... | collective-permute-start | bytes 1572872 | tf_op jit(solution)/shard_map/ppermute | solution.py:54
  183.8 12.4 %collective-permute-start.30 = (bf16[2,1,256,1024]{3,2,1,0:T(8,128)(2,1)}, bf16[2,1,256,1024]{3,2,1,0:T(8,128)(2,1)}, u32[]{:S(2)}, u32[]{:S(2)}) collective-permute-start(bf16[2,1,256,1024]{3,2,1,0:T(8,128)(2,1)} %maximum_select_fusion.9), channel_id=1, source_target_pairs={{0,1},{1,0},{2,3},{3,2},{4,5},{5,4},{6,7},{7,6},{8,9},{9,8},{10,11... | collective-permute-start | bytes 3145736 | tf_op jit(solution)/shard_map/ppermute | solution.py:54
  193.1 9.2 %collective-permute-start.26 = (bf16[2,1,256,1024]{3,2,1,0:T(8,128)(2,1)}, bf16[2,1,256,1024]{3,2,1,0:T(8,128)(2,1)}, u32[]{:S(2)}, u32[]{:S(2)}) collective-permute-start(bf16[2,1,256,1024]{3,2,1,0:T(8,128)(2,1)} %maximum_select_fusion.8), channel_id=1, source_target_pairs={{0,1},{1,0},{2,3},{3,2},{4,5},{5,4},{6,7},{7,6},{8,9},{9,8},{10,11... | collective-permute-start | bytes 3145736 | tf_op jit(solution)/shard_map/ppermute | solution.py:54
  214.1 16.5 %copy-start.22 = (f32[1024,1024]{1,0:T(8,128)}, f32[1024,1024]{1,0:T(8,128)S(1)}, u32[]{:S(2)}) copy-start(f32[1024,1024]{1,0:T(8,128)S(1)} %fusion.6) | copy-start | bytes 12582916
  230.0 27.6 %collective-permute-start.31 = (bf16[2,256,1024]{2,1,0:T(8,128)(2,1)}, bf16[2,256,1024]{2,1,0:T(8,128)(2,1)}, u32[]{:S(2)}, u32[]{:S(2)}) collective-permute-start(bf16[2,256,1024]{2,1,0:T(8,128)(2,1)} %fusion.38), channel_id=1, source_target_pairs={{0,1},{1,0},{2,3},{3,2},{4,5},{5,4},{6,7},{7,6},{8,9},{9,8},{10,11... | collective-permute-start | bytes 3145736 | tf_op jit(solution)/shard_map/ppermute | solution.py:54
  231.8 29.5 %collective-permute-start.27 = (bf16[2,256,1024]{2,1,0:T(8,128)(2,1)}, bf16[2,256,1024]{2,1,0:T(8,128)(2,1)}, u32[]{:S(2)}, u32[]{:S(2)}) collective-permute-start(bf16[2,256,1024]{2,1,0:T(8,128)(2,1)} %fusion.37), channel_id=1, source_target_pairs={{0,1},{1,0},{2,3},{3,2},{4,5},{5,4},{6,7},{7,6},{8,9},{9,8},{10,11... | collective-permute-start | bytes 3145736 | tf_op jit(solution)/shard_map/ppermute | solution.py:54
  255.5 28.4 %collective-permute-start.47 = (bf16[2,1,128,2304]{3,2,1,0:T(8,128)(2,1)S(1)}, bf16[2,1,128,2304]{3,2,1,0:T(8,128)(2,1)S(1)}, u32[]{:S(2)}, u32[]{:S(2)}) collective-permute-start(bf16[2,1,128,2304]{3,2,1,0:T(8,128)(2,1)S(1)} %pad_maximum_fusion.2), channel_id=1, source_target_pairs={{0,8},{1,9},{2,10},{3,11},{4,12},{5,13},{6,14},{7,15},{8,0},{9,1},... | collective-permute-start | bytes 3538952 | tf_op jit(solution)/shard_map/ppermute | solution.py:54
  256.8 28.0 %collective-permute-start.49 = (bf16[2,1,128,2304]{3,2,1,0:T(8,128)(2,1)S(1)}, bf16[2,1,128,2304]{3,2,1,0:T(8,128)(2,1)S(1)}, u32[]{:S(2)}, u32[]{:S(2)}) collective-permute-start(bf16[2,1,128,2304]{3,2,1,0:T(8,128)(2,1)S(1)} %stack.81), channel_id=1, source_target_pairs={{0,16},{1,17},{2,18},{3,19},{4,20},{5,21},{6,22},{7,23},{8,24},{9,... | collective-permute-start | bytes 3538952 | tf_op jit(solution)/shard_map/ppermute | solution.py:54
  259.8 31.0 %collective-permute-start.32 = (bf16[256,1024]{1,0:T(8,128)(2,1)S(1)}, bf16[256,1024]{1,0:T(8,128)(2,1)S(1)}, u32[]{:S(2)}, u32[]{:S(2)}) collective-permute-start(bf16[256,1024]{1,0:T(8,128)(2,1)S(1)} %fusion.89), channel_id=1, source_target_pairs={{0,2},{1,3},{2,0},{3,1},{4,6},{5,7},{6,4},{7,5},{8,10},{9,11},{10,... | collective-permute-start | bytes 1572872 | tf_op jit(solution)/shard_map/ppermute | solution.py:54
  263.2 20.9 %copy-start.14 = (f32[2,256,1024]{2,1,0:T(8,128)}, f32[2,256,1024]{2,1,0:T(8,128)S(1)}, u32[]{:S(2)}) copy-start(f32[2,256,1024]{2,1,0:T(8,128)S(1)} %bitcast_add_fusion.2) | copy-start | bytes 6291460
  264.2 48.5 %collective-permute-start.28 = (bf16[256,1024]{1,0:T(8,128)(2,1)}, bf16[256,1024]{1,0:T(8,128)(2,1)}, u32[]{:S(2)}, u32[]{:S(2)}) collective-permute-start(bf16[256,1024]{1,0:T(8,128)(2,1)} %fusion.87), channel_id=1, source_target_pairs={{0,2},{1,3},{2,0},{3,1},{4,6},{5,7},{6,4},{7,5},{8,10},{9,11},{10,... | collective-permute-start | bytes 1572872 | tf_op jit(solution)/shard_map/ppermute | solution.py:54
  288.8 63.9 %collective-permute-start.50 = (bf16[1,128,2304]{2,1,0:T(8,128)(2,1)}, bf16[1,128,2304]{2,1,0:T(8,128)(2,1)}, u32[]{:S(2)}, u32[]{:S(2)}) collective-permute-start(bf16[1,128,2304]{2,1,0:T(8,128)(2,1)} %get-tuple-element.21), channel_id=1, source_target_pairs={{0,8},{1,9},{2,10},{3,11},{4,12},{5,13},{6,14},{7,15},{8,0},{9,1},... | collective-permute-start | bytes 1769480 | tf_op jit(solution)/shard_map/ppermute | solution.py:54
  289.9 127.3 %collective-permute-start.48 = (bf16[1,128,2304]{2,1,0:T(8,128)(2,1)}, bf16[1,128,2304]{2,1,0:T(8,128)(2,1)}, u32[]{:S(2)}, u32[]{:S(2)}) collective-permute-start(bf16[1,128,2304]{2,1,0:T(8,128)(2,1)} %get-tuple-element.20), channel_id=1, source_target_pairs={{0,16},{1,17},{2,18},{3,19},{4,20},{5,21},{6,22},{7,23},{8,24},{9,... | collective-permute-start | bytes 1769480 | tf_op jit(solution)/shard_map/ppermute | solution.py:54
  345.0 7.5 %collective-permute-start.33 = (bf16[2,2,256,128]{2,3,1,0:T(8,128)(2,1)S(1)}, bf16[2,2,256,128]{2,3,1,0:T(8,128)(2,1)S(1)}, u32[]{:S(2)}, u32[]{:S(2)}) collective-permute-start(bf16[2,2,256,128]{2,3,1,0:T(8,128)(2,1)S(1)} %select_bitcast_fusion.3), channel_id=1, source_target_pairs={{0,2},{1,3},{2,0},{3,1},{4,6},{5,7},{6,4},{7,5},{8,10},{9,11},{10,... | collective-permute-start | bytes 786440 | tf_op jit(solution)/shard_map/ppermute | solution.py:54
  349.8 69.7 %collective-permute-start.38 = (bf16[2,1024,256]{1,2,0:T(8,128)(2,1)}, bf16[2,1024,256]{1,2,0:T(8,128)(2,1)}, u32[]{:S(2)}, u32[]{:S(2)}) collective-permute-start(bf16[2,1024,256]{1,2,0:T(8,128)(2,1)} %fusion.40), channel_id=1, source_target_pairs={{0,1},{1,0},{2,3},{3,2},{4,5},{5,4},{6,7},{7,6},{8,9},{9,8},{10,11... | collective-permute-start | bytes 3145736 | tf_op jit(solution)/shard_map/ppermute | solution.py:54
  352.7 7.2 %collective-permute-start.34 = (bf16[2,2,256,128]{2,3,1,0:T(8,128)(2,1)S(1)}, bf16[2,2,256,128]{2,3,1,0:T(8,128)(2,1)S(1)}, u32[]{:S(2)}, u32[]{:S(2)}) collective-permute-start(bf16[2,2,256,128]{2,3,1,0:T(8,128)(2,1)S(1)} %select_bitcast_fusion.2), channel_id=1, source_target_pairs={{0,1},{1,0},{2,3},{3,2},{4,5},{5,4},{6,7},{7,6},{8,9},{9,8},{10,11... | collective-permute-start | bytes 786440 | tf_op jit(solution)/shard_map/ppermute | solution.py:54
  355.4 61.9 %collective-permute-start.51 = (bf16[128,2304]{1,0:T(8,128)(2,1)}, bf16[128,2304]{1,0:T(8,128)(2,1)}, u32[]{:S(2)}, u32[]{:S(2)}) collective-permute-start(bf16[128,2304]{1,0:T(8,128)(2,1)} %fusion.80), channel_id=1, source_target_pairs={{0,4},{1,5},{2,6},{3,7},{4,0},{5,1},{6,2},{7,3},{8,12},{9,13},{10,... | collective-permute-start | bytes 1769480 | tf_op jit(solution)/shard_map/ppermute | solution.py:54
  363.3 28.8 %collective-permute-start.35 = (f32[2,128,128]{2,1,0:T(8,128)S(1)}, f32[2,128,128]{2,1,0:T(8,128)S(1)}, u32[]{:S(2)}, u32[]{:S(2)}) collective-permute-start(f32[2,128,128]{2,1,0:T(8,128)S(1)} %get-tuple-element.14), channel_id=1, source_target_pairs={{4,0},{5,1},{6,2},{7,3},{12,8},{13,9},{14,10},{15,11},{20,16},{21,... | collective-permute-start | bytes 393224 | tf_op jit(solution)/shard_map/ppermute | solution.py:74
  365.4 26.7 %copy-start.65 = (f32[2]{0:T(128)S(1)}, f32[2]{0:T(128)}, u32[]{:S(2)}) copy-start(f32[2]{0:T(128)} %get-tuple-element.16) | copy-start | bytes 28
  365.4 26.7 %copy-start.67 = (f32[2]{0:T(128)S(1)}, f32[2]{0:T(128)}, u32[]{:S(2)}) copy-start(f32[2]{0:T(128)} %get-tuple-element.79) | copy-start | bytes 28
  406.5 48.9 %collective-permute-start.36 = (bf16[2,256,1024]{2,1,0:T(8,128)(2,1)}, bf16[2,256,1024]{2,1,0:T(8,128)(2,1)}, u32[]{:S(2)}, u32[]{:S(2)}) collective-permute-start(bf16[2,256,1024]{2,1,0:T(8,128)(2,1)} %fusion.39), channel_id=1, source_target_pairs={{0,1},{1,0},{2,3},{3,2},{4,5},{5,4},{6,7},{7,6},{8,9},{9,8},{10,11... | collective-permute-start | bytes 3145736 | tf_op jit(solution)/shard_map/ppermute | solution.py:54
  419.3 9.9 %collective-permute-start.52 = (bf16[2,32,2304]{2,1,0:T(8,128)(2,1)S(1)}, bf16[2,32,2304]{2,1,0:T(8,128)(2,1)S(1)}, u32[]{:S(2)}, u32[]{:S(2)}) collective-permute-start(bf16[2,32,2304]{2,1,0:T(8,128)(2,1)S(1)} %bitcast.670), channel_id=1, source_target_pairs={{0,2},{1,3},{2,0},{3,1},{4,6},{5,7},{6,4},{7,5},{8,10},{9,11},{10,... | collective-permute-start | bytes 884744 | tf_op jit(solution)/shard_map/ppermute | solution.py:54
  422.9 17.1 %collective-permute-start.39 = (bf16[1024,256]{0,1:T(8,128)(2,1)}, bf16[1024,256]{0,1:T(8,128)(2,1)}, u32[]{:S(2)}, u32[]{:S(2)}) collective-permute-start(bf16[1024,256]{0,1:T(8,128)(2,1)} %fusion.91), channel_id=1, source_target_pairs={{0,2},{1,3},{2,0},{3,1},{4,6},{5,7},{6,4},{7,5},{8,10},{9,11},{10,... | collective-permute-start | bytes 1572872 | tf_op jit(solution)/shard_map/ppermute | solution.py:54
  429.5 1.6 collective-permute-start.53
  458.2 13.4 %collective-permute-start.37 = (bf16[256,1024]{1,0:T(8,128)(2,1)S(1)}, bf16[256,1024]{1,0:T(8,128)(2,1)S(1)}, u32[]{:S(2)}, u32[]{:S(2)}) collective-permute-start(bf16[256,1024]{1,0:T(8,128)(2,1)S(1)} %fusion.90), channel_id=1, source_target_pairs={{0,2},{1,3},{2,0},{3,1},{4,6},{5,7},{6,4},{7,5},{8,10},{9,11},{10,... | collective-permute-start | bytes 1572872 | tf_op jit(solution)/shard_map/ppermute | solution.py:54
  458.7 19.6 %collective-permute-start.40 = (bf16[2,1,128,1280]{3,2,1,0:T(8,128)(2,1)S(1)}, bf16[2,1,128,1280]{3,2,1,0:T(8,128)(2,1)}, u32[]{:S(2)}, u32[]{:S(2)}) collective-permute-start(bf16[2,1,128,1280]{3,2,1,0:T(8,128)(2,1)S(1)} %pad_maximum_fusion.5), channel_id=1, source_target_pairs={{0,8},{1,9},{2,10},{3,11},{4,12},{5,13},{6,14},{7,15},{8,0},{9,1},... | collective-permute-start | bytes 1966088 | tf_op jit(solution)/shard_map/ppermute | solution.py:54
  459.6 19.9 %collective-permute-start.42 = (bf16[2,1,128,1280]{3,2,1,0:T(8,128)(2,1)S(1)}, bf16[2,1,128,1280]{3,2,1,0:T(8,128)(2,1)}, u32[]{:S(2)}, u32[]{:S(2)}) collective-permute-start(bf16[2,1,128,1280]{3,2,1,0:T(8,128)(2,1)S(1)} %stack.80), channel_id=1, source_target_pairs={{0,16},{1,17},{2,18},{3,19},{4,20},{5,21},{6,22},{7,23},{8,24},{9,... | collective-permute-start | bytes 1966088 | tf_op jit(solution)/shard_map/ppermute | solution.py:54
  482.3 8.4 %collective-permute-start.43 = (bf16[1,128,1280]{2,1,0:T(8,128)(2,1)S(1)}, bf16[1,128,1280]{2,1,0:T(8,128)(2,1)S(1)}, u32[]{:S(2)}, u32[]{:S(2)}) collective-permute-start(bf16[1,128,1280]{2,1,0:T(8,128)(2,1)S(1)} %get-tuple-element.23), channel_id=1, source_target_pairs={{0,8},{1,9},{2,10},{3,11},{4,12},{5,13},{6,14},{7,15},{8,0},{9,1},... | collective-permute-start | bytes 983048 | tf_op jit(solution)/shard_map/ppermute | solution.py:54
  483.2 15.0 %collective-permute-start.41 = (bf16[1,128,1280]{2,1,0:T(8,128)(2,1)S(1)}, bf16[1,128,1280]{2,1,0:T(8,128)(2,1)S(1)}, u32[]{:S(2)}, u32[]{:S(2)}) collective-permute-start(bf16[1,128,1280]{2,1,0:T(8,128)(2,1)S(1)} %get-tuple-element.22), channel_id=1, source_target_pairs={{0,16},{1,17},{2,18},{3,19},{4,20},{5,21},{6,22},{7,23},{8,24},{9,... | collective-permute-start | bytes 983048 | tf_op jit(solution)/shard_map/ppermute | solution.py:54
  492.6 15.7 %collective-permute-start.44 = (bf16[128,1280]{1,0:T(8,128)(2,1)}, bf16[128,1280]{1,0:T(8,128)(2,1)}, u32[]{:S(2)}, u32[]{:S(2)}) collective-permute-start(bf16[128,1280]{1,0:T(8,128)(2,1)} %fusion.96), channel_id=1, source_target_pairs={{0,4},{1,5},{2,6},{3,7},{4,0},{5,1},{6,2},{7,3},{8,12},{9,13},{10,... | collective-permute-start | bytes 983048 | tf_op jit(solution)/shard_map/ppermute | solution.py:54
  509.6 5.6 %collective-permute-start.45 = (bf16[2,32,1280]{2,1,0:T(8,128)(2,1)S(1)}, bf16[2,32,1280]{2,1,0:T(8,128)(2,1)S(1)}, u32[]{:S(2)}, u32[]{:S(2)}) collective-permute-start(bf16[2,32,1280]{2,1,0:T(8,128)(2,1)S(1)} %bitcast.680), channel_id=1, source_target_pairs={{0,2},{1,3},{2,0},{3,1},{4,6},{5,7},{6,4},{7,5},{8,10},{9,11},{10,... | collective-permute-start | bytes 491528 | tf_op jit(solution)/shard_map/ppermute | solution.py:54
  515.3 1.5 collective-permute-start.46
  (61 other events, 197.3 us)
